TPU v7x, 256 devices: a whole 4x4x8 slice. The times are simulated.
256 devices in a mesh: seq: 32 (over z, x_lo, core), chan: 8 (over x_hi, y).
Axes of the slice: x: 4 (x_hi: 2, x_lo: 2; x = x_hi * 2 + x_lo), y: 4, z: 8, core: 2. Of those that a mesh axis runs over, the one named last changes fastest.
Arguments:
- tokens: bfloat16 [8192, 4096], P('seq'), may hold values from -6 to 6
- w_in: bfloat16 [4096, 3, 4096], P('seq', None, 'chan'), may hold values from -0.09375 to 0.09375
- short_taps: float32 [3, 3, 4096], P(None, None, 'chan'), may hold values from -3.5 to 3.5
- residues: float32 [16, 4096], P(None, 'chan'), may hold values from -6 to 6
- decay_rates: float32 [16, 4096], P(None, 'chan'), may hold values from 3.0517578e-05 to 0.05
- skip_gain: float32 [4096], P('chan'), may hold values from -4 to 4
- w_out: bfloat16 [4096, 4096], P('chan'), may hold values from -0.125 to 0.125
Outputs:
- operator_out: bfloat16 [8192, 4096], P('seq', 'chan')
All inputs are finite; a program needn't handle non-finite values.
Results may differ from a plain program's by a relative error of at most 0.015.
Values may be sent and summed in bfloat16 or wider, within the bound.
A program may use at most 128 MiB of HBM per device.

v0:
```python
import math

import jax
import jax.numpy as jnp
from jax import lax
from jax.sharding import PartitionSpec as P

HIGHEST = lax.Precision.HIGHEST


def passed_along(block, axis, distance):
    devices = range(lax.axis_size(axis))
    route = [(i - distance, i) for i in devices if i - distance in devices]
    return lax.ppermute(block, axis, route)


def unit_circle(numerator, divisor):
    angles = (numerator % divisor).astype(jnp.float32) * (2.0 * math.pi / divisor)
    return (jnp.cos(angles), jnp.sin(angles))


def regroup(block):
    return lax.all_to_all(block, "seq", split_axis=1, concat_axis=0, tiled=True)


def forward_spectrum(signal, slab_index, seq_count, square_cos, square_sin):
    tok_rows, stream_count, chan_width = signal.shape
    pieces = tok_rows // seq_count
    outer_len = 2 * seq_count
    whole_len = outer_len * tok_rows
    spread = regroup(signal.reshape(1, tok_rows, stream_count * chan_width))
    outer_pos = jnp.arange(outer_len, dtype=jnp.int32)
    inner_pos = jnp.arange(seq_count, dtype=jnp.int32)
    outer_cos, outer_sin = unit_circle(outer_pos[:, None] * inner_pos[None, :], outer_len)
    real_part = jnp.einsum("kn,njc->jkc", outer_cos, spread, precision=HIGHEST)
    imag_part = -jnp.einsum("kn,njc->jkc", outer_sin, spread, precision=HIGHEST)
    local_rows = slab_index * pieces + jnp.arange(pieces, dtype=jnp.int32)
    twist_cos, twist_sin = unit_circle(local_rows[:, None] * outer_pos[None, :], whole_len)
    twist_cos = twist_cos[:, :, None]
    twist_sin = twist_sin[:, :, None]
    turned_real = real_part * twist_cos + imag_part * twist_sin
    turned_imag = imag_part * twist_cos - real_part * twist_sin
    packed = jnp.stack([turned_real, turned_imag], 2).reshape(
        pieces, outer_len, 2 * stream_count * chan_width
    )
    gathered = regroup(packed).reshape(tok_rows, 2, 2, stream_count * chan_width)
    part_real = gathered[:, :, 0].reshape(tok_rows, -1)
    part_imag = gathered[:, :, 1].reshape(tok_rows, -1)
    spec_real = jnp.dot(square_cos, part_real, precision=HIGHEST) + jnp.dot(
        square_sin, part_imag, precision=HIGHEST
    )
    spec_imag = jnp.dot(square_cos, part_imag, precision=HIGHEST) - jnp.dot(
        square_sin, part_real, precision=HIGHEST
    )
    spec_shape = (tok_rows, 2, stream_count, chan_width)
    return (spec_real.reshape(spec_shape), spec_imag.reshape(spec_shape))


def inverse_signal(mixed_real, mixed_imag, slab_index, seq_count, square_cos, square_sin):
    tok_rows, _, chan_width = mixed_real.shape
    pieces = tok_rows // seq_count
    outer_len = 2 * seq_count
    whole_len = outer_len * tok_rows
    real_part = jnp.einsum("mk,krc->rmc", square_cos, mixed_real, precision=HIGHEST) - jnp.einsum(
        "mk,krc->rmc", square_sin, mixed_imag, precision=HIGHEST
    )
    imag_part = jnp.einsum("mk,krc->rmc", square_cos, mixed_imag, precision=HIGHEST) + jnp.einsum(
        "mk,krc->rmc", square_sin, mixed_real, precision=HIGHEST
    )
    outer_local = 2 * slab_index + jnp.arange(2, dtype=jnp.int32)
    positions = jnp.arange(tok_rows, dtype=jnp.int32)
    twist_cos, twist_sin = unit_circle(outer_local[:, None] * positions[None, :], whole_len)
    twist_cos = twist_cos[:, :, None]
    twist_sin = twist_sin[:, :, None]
    turned_real = real_part * twist_cos - imag_part * twist_sin
    turned_imag = real_part * twist_sin + imag_part * twist_cos
    packed = jnp.stack([turned_real, turned_imag], 2).reshape(2, tok_rows, 2 * chan_width)
    gathered = regroup(packed).reshape(outer_len, pieces, 2, chan_width)
    outer_pos = jnp.arange(outer_len, dtype=jnp.int32)
    inner_pos = jnp.arange(seq_count, dtype=jnp.int32)
    outer_cos, outer_sin = unit_circle(inner_pos[:, None] * outer_pos[None, :], outer_len)
    factor = 1.0 / whole_len
    restored = jnp.einsum(
        "nk,kjc->jnc", outer_cos * factor, gathered[:, :, 0], precision=HIGHEST
    ) - jnp.einsum("nk,kjc->jnc", outer_sin * factor, gathered[:, :, 1], precision=HIGHEST)
    return regroup(restored).reshape(tok_rows, chan_width)


def body(tokens, w_in, short_taps, residues, decay_rates, skip_gain, w_out):
    tok_rows = tokens.shape[0]
    chan_width = w_in.shape[2]
    seq_count = lax.axis_size("seq")
    slab_index = lax.axis_index("seq")
    w_piece = lax.all_gather(w_in, "seq", axis=0, tiled=True)
    projected = jnp.dot(
        tokens, w_piece.reshape(w_piece.shape[0], -1), preferred_element_type=jnp.float32
    )
    streams = projected.astype(jnp.bfloat16).reshape(tok_rows, 3, chan_width)
    before = passed_along(streams[tok_rows - 2 :], "seq", 1)
    extended = jnp.concatenate([before, streams], 0).astype(jnp.float32)
    shorted = (
        short_taps[0] * extended[2:]
        + short_taps[1] * extended[1 : tok_rows + 1]
        + short_taps[2] * extended[:tok_rows]
    )
    product = shorted[:, 1] * shorted[:, 2]
    amplitude = residues * jnp.sqrt(2.0 * decay_rates / residues.shape[0])
    positions = jnp.arange(tok_rows, dtype=jnp.int32)
    square_cos, square_sin = unit_circle(positions[:, None] * positions[None, :], tok_rows)
    times_global = (slab_index * tok_rows + positions).astype(jnp.float32)
    kernel = jnp.sum(
        amplitude[None] * jnp.exp(-(decay_rates[None] * times_global[:, None, None])), 1
    )
    spec_real, spec_imag = forward_spectrum(
        jnp.stack([product, kernel], 1), slab_index, seq_count, square_cos, square_sin
    )
    sig_real = spec_real[:, :, 0]
    sig_imag = spec_imag[:, :, 0]
    filt_real = spec_real[:, :, 1]
    filt_imag = spec_imag[:, :, 1]
    mixed_real = sig_real * filt_real - sig_imag * filt_imag
    mixed_imag = sig_real * filt_imag + sig_imag * filt_real
    long_conv = inverse_signal(
        mixed_real, mixed_imag, slab_index, seq_count, square_cos, square_sin
    )
    gated_out = (shorted[:, 0] * (long_conv + skip_gain * product)).astype(jnp.bfloat16)
    partial_value = jnp.dot(gated_out, w_out, preferred_element_type=jnp.float32)
    return lax.psum_scatter(
        partial_value.astype(jnp.bfloat16), "chan", scatter_dimension=1, tiled=True
    )


def solution(mesh):
    return jax.shard_map(
        body,
        mesh=mesh,
        in_specs=(
            P("seq", None),
            P("seq", None, "chan"),
            P(None, None, "chan"),
            P(None, "chan"),
            P(None, "chan"),
            P("chan"),
            P("chan", None),
        ),
        out_specs=P("seq", "chan"),
        check_vma=False,
    )
```

profile of v0, /device:TPU:1, one launch (start us, length us, event | category | flops | bytes accessed | tf_op | source)
XLA Modules:
  0.0 559.4 jit_solution(343387621256798042)
XLA Ops:
  6.5 2.1 copy.97
  9.5 3.2 multiply_reduce_fusion
  12.7 107.7 %all-gather.2.cloned.1.call-done = bf16[4096,3,512]{0,2,1:T(8,128)(2,1)} async-done(((bf16[128,3,512]{0,2,1:T(8,128)(2,1)}), bf16[4096,3,512]{0,2,1:T(8,128)(2,1)}) %all-gather.2.cloned.1.call-update) | async-done | bytes 12582928 | tf_op jit(solution)/shard_map/all_gather | solution.py:94
  120.4 6.5 %convolution_convert_fusion.1 = bf16[256,1536]{1,0:T(8,128)(2,1)S(1)} fusion(bf16[256,4096]{1,0:T(8,128)(2,1)S(1)} %copy-done, bf16[4096,1536]{0,1:T(8,128)(2,1)} %bitcast.137), kind=kOutput, calls=%fused_computation.6 | convolution fusion | flops 3221618688 | bytes 15466496 | tf_op jit(solution)/shard_map/dot_general | solution.py:95
  127.0 4.5 collective-permute-start
  133.0 1.2 copy-done.4
  134.6 2.0 copy.102
  136.6 7.4 %all-to-all-start = ((f32[1,256,1024]{2,0,1:T(1,128)}), f32[1,256,1024]{2,0,1:T(1,128)S(1)}, u32[]{:S(2)}, u32[]{:S(2)}) async-start(f32[1,256,1024]{2,0,1:T(1,128)} %copy.102), calls=%async_computation | async-start | bytes 2097152 | tf_op jit(solution)/shard_map/all_to_all | solution.py:23
  144.1 27.9 %all-to-all-done = f32[1,256,1024]{2,0,1:T(1,128)S(1)} async-done(((f32[1,256,1024]{2,0,1:T(1,128)}), f32[1,256,1024]{2,0,1:T(1,128)S(1)}, u32[]{:S(2)}, u32[]{:S(2)}) %all-to-all-start) | async-done | bytes 1048608 | tf_op jit(solution)/shard_map/all_to_all | solution.py:23
  172.2 2.6 fusion.10
  174.8 3.2 add_bitcast_fusion
  178.6 5.2 copy.121
  183.8 6.7 %reshape.182 = f32[8,64,2048]{2,0,1:T(8,128)} reshape(f32[8,64,2,1024]{3,2,0,1:T(2,128)} %copy.121) | data formatting | bytes 8388608 | tf_op jit(solution)/shard_map/reshape | solution.py:43
  190.5 5.6 %all-to-all-start.1 = ((f32[8,64,2048]{2,0,1:T(8,128)}), f32[8,64,2048]{2,0,1:T(8,128)}, u32[]{:S(2)}, u32[]{:S(2)}) async-start(f32[8,64,2048]{2,0,1:T(8,128)} %reshape.182), calls=%async_computation.1 | async-start | bytes 8388608 | tf_op jit(solution)/shard_map/all_to_all | solution.py:23
  196.7 93.4 %all-to-all-done.1 = f32[8,64,2048]{2,0,1:T(8,128)} async-done(((f32[8,64,2048]{2,0,1:T(8,128)}), f32[8,64,2048]{2,0,1:T(8,128)}, u32[]{:S(2)}, u32[]{:S(2)}) %all-to-all-start.1) | async-done | bytes 4194336 | tf_op jit(solution)/shard_map/all_to_all | solution.py:23
  290.2 4.7 copy.143
  294.9 6.6 %reshape.170 = f32[256,2,2,1024]{3,2,0,1:T(2,128)} reshape(f32[32,8,2,2048]{3,1,0,2:T(8,128)} %bitcast.128) | data formatting | bytes 8388608 | tf_op jit(solution)/shard_map/reshape | solution.py:46
  301.4 9.1 %fusion.131 = (f32[256,2,1,1024]{3,2,0,1:T(1,128)}, f32[256,2,1,1024]{3,2,0,1:T(1,128)}) fusion(f32[256,2,2,1024]{3,2,0,1:T(2,128)} %reshape.170), kind=kLoop, calls=%fused_computation.170 | loop fusion | bytes 8388608 | tf_op jit(solution)/shard_map/slice | solution.py:47
  310.5 4.6 copy.108
  315.1 4.2 fusion.34
  319.3 6.2 %copy.109 = f32[256,2,1,1024]{0,3,1,2:T(8,128)} copy(f32[256,2,1,1024]{3,2,0,1:T(1,128)} %get-tuple-element.10) | data formatting | bytes 4194304 | tf_op jit(solution)/shard_map/slice | solution.py:48
  325.5 5.9 %fusion.32 = f32[256,2048]{1,0:T(8,128)} fusion(f32[256,2048]{0,1:T(8,128)} %bitcast.126), kind=kOutput, calls=%fused_computation.62 | convolution fusion | flops 1611530240 | bytes 4194304 | tf_op jit(solution)/shard_map/dot_general | solution.py:52
  331.4 4.3 convolution_add_fusion
  335.7 4.0 reshape.171
  339.7 5.3 fusion.134
  345.1 3.6 copy.124
  348.7 3.6 copy.125
  352.3 5.8 %convolution_subtract_fusion = f32[256,2048]{1,0:T(8,128)} fusion(f32[256,2048]{1,0:T(8,128)} %fusion.32, f32[256,2048]{0,1:T(8,128)S(1)} %bitcast.125), kind=kOutput, calls=%fused_computation.4 | convolution fusion | flops 1612054528 | bytes 6291456 | tf_op jit(solution)/shard_map/dot_general | solution.py:52
  358.1 3.2 reshape.172
  361.3 3.0 fusion.133
  364.3 3.7 copy.126
  368.0 2.1 copy.127
  370.1 2.4 multiply_subtract_fusion
  372.5 2.0 fusion.4
  374.5 2.0 fusion.8
  376.5 2.0 convolution_add_fusion.1
  378.5 2.1 subtract_bitcast_fusion.1
  380.8 1.5 copy.114
  382.3 3.2 copy.115
  385.5 56.4 %all_to_all.57 = f32[2,256,1024]{2,0,1:T(2,128)S(1)} all-to-all(f32[2,256,1024]{2,0,1:T(2,128)S(1)} %copy.115), channel_id=1, replica_groups=mesh['seq'=32,'chan'=8] {'seq'}, dimensions={1} | all-to-all | bytes 4194304 | tf_op jit(solution)/shard_map/all_to_all | solution.py:23
  442.5 1.6 copy.117
  444.1 3.0 reshape.174
  447.2 2.4 fusion.132
  449.6 1.3 fusion.3
  450.9 1.3 fusion.2
  452.6 20.8 %all_to_all.58 = f32[8,32,512]{2,0,1:T(8,128)S(1)} all-to-all(f32[8,32,512]{2,0,1:T(8,128)S(1)} %copy.120), channel_id=1, replica_groups=mesh['seq'=32,'chan'=8] {'seq'}, dimensions={1} | all-to-all | bytes 1048576 | tf_op jit(solution)/shard_map/all_to_all | solution.py:23
  473.4 3.8 convolution_convert_fusion
  477.2 74.9 %reduce-scatter.2.cloned.1.call-done = bf16[256,512]{1,0:T(8,128)(2,1)} async-done(((bf16[256,4096]{1,0:T(8,128)(2,1)}), bf16[256,512]{1,0:T(8,128)(2,1)}) %reduce-scatter.2.cloned.1.call-update) | async-done | bytes 262160 | tf_op jit(solution)/shard_map/reduce_scatter | solution.py:128
  (42 shorter events, 5.3 us)
Async XLA Ops:
  6.5 113.9 %copy-start = (bf16[256,4096]{1,0:T(8,128)(2,1)S(1)}, bf16[256,4096]{1,0:T(8,128)(2,1)}, u32[]{:S(2)}) copy-start(bf16[256,4096]{1,0:T(8,128)(2,1)} %param.7) | copy-start | bytes 6291460
  6.5 113.9 %all-gather.2.cloned.1.call-start = ((), (), s32[]{:S(2)}) async-start(), calls=%async_computation.5 | async-start | bytes 12976128 | tf_op jit(solution)/shard_map/all_gather | solution.py:94
  120.4 11.1 %copy-start.7 = (f32[3,3,512]{2,1,0:T(4,128)S(1)}, f32[3,3,512]{2,1,0:T(4,128)}, u32[]{:S(2)}) copy-start(f32[3,3,512]{2,1,0:T(4,128)} %param.9) | copy-start | bytes 55300
  127.0 5.3 collective-permute-start
  132.9 1.2 copy-start.4
  136.6 35.4 %all-to-all-start = ((f32[1,256,1024]{2,0,1:T(1,128)}), f32[1,256,1024]{2,0,1:T(1,128)S(1)}, u32[]{:S(2)}, u32[]{:S(2)}) async-start(f32[1,256,1024]{2,0,1:T(1,128)} %copy.102), calls=%async_computation | async-start | bytes 2097152 | tf_op jit(solution)/shard_map/all_to_all | solution.py:23
  190.5 99.7 %all-to-all-start.1 = ((f32[8,64,2048]{2,0,1:T(8,128)}), f32[8,64,2048]{2,0,1:T(8,128)}, u32[]{:S(2)}, u32[]{:S(2)}) async-start(f32[8,64,2048]{2,0,1:T(8,128)} %reshape.182), calls=%async_computation.1 | async-start | bytes 8388608 | tf_op jit(solution)/shard_map/all_to_all | solution.py:23
  196.1 356.0 %reduce-scatter.2.cloned.1.call-start = ((), (), s32[]{:S(2)}) async-start(), calls=%async_computation.6 | async-start | bytes 2359296 | tf_op jit(solution)/shard_map/reduce_scatter | solution.py:128
  325.5 6.0 %copy-start.2 = (f32[256,2,1,1024]{0,3,1,2:T(8,128)S(1)}, f32[256,2,1,1024]{0,3,1,2:T(8,128)}, u32[]{:S(2)}) copy-start(f32[256,2,1,1024]{0,3,1,2:T(8,128)} %copy.109) | copy-start | bytes 6291460
  325.5 6.0 %copy-start.3 = (f32[256,2048]{1,0:T(8,128)S(1)}, f32[256,2048]{1,0:T(8,128)}, u32[]{:S(2)}) copy-start(f32[256,2048]{1,0:T(8,128)} %fusion.34) | copy-start | bytes 6291460
  364.3 3.7 copy-start.6
  447.2 26.2 %copy-start.8 = (f32[512]{0:T(512)S(1)}, f32[512]{0:T(512)}, u32[]{:S(2)}) copy-start(f32[512]{0:T(512)} %param.12) | copy-start | bytes 6148
  450.9 22.5 %copy-start.5 = (bf16[512,4096]{1,0:T(8,128)(2,1)S(1)}, bf16[512,4096]{1,0:T(8,128)(2,1)}, u32[]{:S(2)}) copy-start(bf16[512,4096]{1,0:T(8,128)(2,1)} %param.13) | copy-start | bytes 12582916
  473.4 78.7 %copy-start.1 = (bf16[256,4096]{1,0:T(8,128)(2,1)S(1)}, bf16[256,4096]{1,0:T(8,128)(2,1)}, u32[]{:S(2)}) copy-start(bf16[256,4096]{1,0:T(8,128)(2,1)} %param.7) | copy-start | bytes 6291460
Sparse Core Ops, SparseCore 0:
  9.1 111.2 all-gather.1
  477.4 74.6 reduce-scatter.1
where the time goes:
time: 565 us; the launch traced here: 559 us
  waiting for transfers between devices  304 us (54%)
  local copies, waits for them, and re-layouts  90.5 us (16%)
  blocking collectives  77.2 us (14%)
  matrix products  47.2 us (8%)
  starting transfers between devices  18 us (3%)
  between operations  14.2 us (3%)
  other arithmetic  8.16 us (1%)
    all_to_all x2, waiting for transfers between devices, regroup(): return lax.all_to_all(block, 'seq', split_axis=1, concat_axis=0, tiled=True)  121 us
    all_gather x1, waiting for transfers between devices, body(): w_piece = lax.all_gather(w_in, 'seq', axis=0, tiled=True)  108 us
    all_to_all x2, blocking collectives, regroup(): return lax.all_to_all(block, 'seq', split_axis=1, concat_axis=0, tiled=True)  77.2 us
    reduce_scatter x1, waiting for transfers between devices, body(): lax.psum_scatter(partial_value.astype(jnp.bfloat16), 'chan', scatter_dime...  74.9 us
    unnamed x24, local copies, waits for them, and re-layouts  16.5 us
    slice x2, local copies, waits for them, and re-layouts, forward_spectrum(): part_real = gathered[:, :, 0].reshape(tok_rows, -1)  13.6 us
    all_to_all x2, starting transfers between devices, regroup(): return lax.all_to_all(block, 'seq', split_axis=1, concat_axis=0, tiled=True)  13 us
    reshape x2, local copies, waits for them, and re-layouts, forward_spectrum(): jnp.stack([turned_real, turned_imag], 2)  11.9 us
  transfers between devices with their start and end apart: 5, of which 5 were waited for; matrix products, arithmetic and copies ran while one was open for 1% of the time, Pallas kernels for 0%

commit v1 on v0

v1 whole, which is shorter than its diff:
```python
import functools

import jax
import jax.numpy as jnp
from jax import lax
from jax.experimental import pallas as pl
from jax.experimental.pallas import tpu as pltpu
from jax.sharding import PartitionSpec as P

MESH = pl.DeviceIdType.MESH
F32, BF16 = jnp.float32, jnp.bfloat16

PLANES = 8
YS = 4
SLABS = 32
CHANS = 8
CHUNKS = 4
LANES = 128
WIDE = 3 * LANES
DEPTH = 4096
BLOCK = DEPTH // SLABS
HALF = BLOCK // 2
ROWS = 256
HALO = 16
SEGS = 8
SEG = ROWS // SEGS
MODES = 16


def copied(ref, sem):
    pltpu.make_async_copy(ref, ref, sem).wait()


def kernel(
    tokens, w_in, taps, residues, decays, skip, w_out, out,
    wbuf, tok, wt, pj, sh0, prod, ylocal, hseg, est, pst, gated, acc,
    local_sem, w_send, w_major, w_minor, w_cross, w_inject, w_core,
    halo_sem, est_send, est_recv, pst_send, pst_recv, gate_send, gate_recv,
    wt_send, wt_recv, wt_core, wt_core_send,
):
    slab, chan = lax.axis_index("seq"), lax.axis_index("chan")
    z, spot = slab // 4, lax.rem(slab, 4)
    x, core = spot // 2, lax.rem(spot, 2)
    xhi, y = chan // YS, lax.rem(chan, YS)
    sign = 1 - 2 * core

    def at(z_, x_, core_, xhi_, y_):
        return (z_ * 4 + x_ * 2 + core_, xhi_ * YS + y_)

    def turned(distance):
        return lax.rem(z + distance * sign + 2 * PLANES, PLANES)

    ahead, behind = at(turned(1), x, core, xhi, y), at(turned(-1), x, core, xhi, y)
    beside, twin = at(z, 1 - x, core, xhi, y), at(z, x, 1 - core, xhi, y)
    across = at(z, x, core, 1 - xhi, y)
    planes = [at(lax.rem(z + d, PLANES), x, core, xhi, y) for d in range(1, PLANES)]
    mates = [at(z, x, 1 - core, xhi, y), at(z, 1 - x, core, xhi, y), at(z, 1 - x, 1 - core, xhi, y)]
    mate_spots = [x * 2 + 1 - core, (1 - x) * 2 + core, (1 - x) * 2 + 1 - core]
    next_slab = (lax.rem(slab + 1, SLABS), chan)
    prev_slab = (lax.rem(slab + SLABS - 1, SLABS), chan)
    y_mates = [lax.rem(y + d, YS) for d in (1, 3, 2)]
    diagonals = [at(z, 1 - x, core, 1 - xhi, y_) for y_ in range(YS)]

    def start(src, dst, send, recv, device):
        pltpu.make_async_remote_copy(
            src_ref=src, dst_ref=dst, send_sem=send, recv_sem=recv, device_id=device, device_id_type=MESH
        ).start()


    def rows(c, z_, x_, core_, first, count):
        begin = pl.multiple_of((z_ * 4 + x_ * 2 + core_) * BLOCK + first, HALF)
        return wbuf.at[c, pl.ds(begin, count)]

    def w_copy(c, ref, device, recv):
        start(ref, ref, w_send.at[c], recv, device)

    def main_rows(c, z_):
        return rows(c, z_, x, core, 0, BLOCK)

    def carried_rows(c, z_):
        return rows(c, z_, 1 - x, core, 0, HALF)

    def to_core(c, ref):
        w_copy(c, ref, twin, w_core.at[c])

    def own_first(c):
        w_copy(c, rows(c, z, x, core, 0, HALF), beside, w_inject.at[c])
        w_copy(c, main_rows(c, z), ahead, w_major.at[c, 0, 0])
        w_copy(c, main_rows(c, z), behind, w_minor.at[c, 0, 0])
        w_copy(c, rows(c, z, x, core, HALF, HALF), beside, w_cross.at[c, 0])
        to_core(c, main_rows(c, z))

    def own_second(c):
        block = carried_rows(c, z)
        copied(block, w_inject.at[c])
        w_copy(c, block, ahead, w_major.at[c, 0, 1])
        w_copy(c, block, behind, w_minor.at[c, 0, 1])
        to_core(c, block)

    def ring(c, j):
        for part, of in ((0, main_rows), (1, carried_rows)):
            for sems, device, last, source, place in (
                (w_major, ahead, 4, turned(-j), j),
                (w_minor, behind, 3, turned(j), 4 + j),
            ):
                if j > last:
                    continue
                block = of(c, source)
                copied(block, sems.at[c, j - 1, part])
                if j < last:
                    w_copy(c, block, device, sems.at[c, j, part])
                if part == 0:
                    w_copy(c, rows(c, source, x, core, HALF, HALF), beside, w_cross.at[c, place])
                to_core(c, block)

    def cross(c, j):
        places = [(z, 0)] if j == 0 else [(turned(-j), j)] + ([(turned(j), 4 + j)] if j < 4 else [])
        for source, place in places:
            block = rows(c, source, 1 - x, core, HALF, HALF)
            copied(block, w_cross.at[c, place])
            to_core(c, block)


    w_out_chunks = w_out.reshape(CHUNKS, LANES, DEPTH)
    mine = pl.ds(core * 2, 2)

    def wt_slot(part, source):
        return wt.at[part, pl.ds(pl.multiple_of(source * LANES, LANES), LANES)]

    def wt_columns(part, target):
        return w_out_chunks.at[part, :, pl.ds(pl.multiple_of(target * 512, 512), 512)]

    wt_peers = [(xhi * YS + y_, at(z, x, core, xhi, y_)) for y_ in y_mates]
    wt_peers += [((1 - xhi) * YS + y_, diagonals[y_]) for y_ in range(YS)]

    def wt_start():
        for target, device in wt_peers:
            start(wt_columns(mine, target), wt_slot(mine, chan), wt_send, wt_recv.at[chan], device)

    def wt_relay():
        for source, _ in wt_peers:
            copied(wt_slot(mine, source), wt_recv.at[source])
            start(wt_slot(mine, source), wt_slot(mine, source), wt_core_send, wt_core, twin)


    def lanes(ref, row, c):
        return ref[pl.ds(row, 1), c * LANES:(c + 1) * LANES]

    def wait_w(c):
        copied(wbuf.at[c, pl.ds(0, DEPTH // 2)], w_core.at[c])

    def project(c):
        result = jnp.dot(tok[...], wbuf[c], preferred_element_type=F32)
        pj[...] = result.astype(BF16).astype(F32)

        @pl.when(slab == 0)
        def _():
            pj[pl.ds(0, HALO)] = jnp.zeros((HALO, WIDE), F32)

    def shorten(c):
        def stream(j):
            total = None
            for a in range(3):
                term = lanes(taps, a * 3 + j, c) * pj[pl.ds(HALO - a, ROWS), j * LANES:(j + 1) * LANES]
                total = term if total is None else total + term
            return total

        sh0[c] = stream(0)
        prod[c] = stream(1) * stream(2)

    def mode_lanes(c, m):
        rate = jnp.broadcast_to(lanes(decays, m, c), (SEGS, LANES))
        size = jnp.broadcast_to(lanes(residues, m, c), (SEGS, LANES))
        return rate, size

    def recur(c):
        factors, gains = [], []
        for m in range(MODES):
            rate, size = mode_lanes(c, m)
            factors.append(jnp.exp(-rate))
            gains.append(size * jnp.sqrt(rate * (2.0 / MODES)))

        def step(i, states):
            value = prod[c, pl.ds(i, SEGS, stride=SEG), :]
            states = tuple(f * s + g * value for f, g, s in zip(factors, gains, states))
            parts = list(states)
            while len(parts) > 1:
                parts = [a + b for a, b in zip(parts[::2], parts[1::2])]
            ylocal[c, pl.ds(i, SEGS, stride=SEG), :] = parts[0]
            return states

        states = lax.fori_loop(0, SEG, step, (jnp.zeros((SEGS, LANES), F32),) * MODES, unroll=4)
        segment = lax.broadcasted_iota(jnp.int32, (SEGS, LANES), 0)
        for m in range(MODES):
            rate, _ = mode_lanes(c, m)
            total = states[m]
            for shift in (1, 2, 4):
                earlier = jnp.where(segment >= shift, pltpu.roll(total, shift, 0), 0.0)
                total = total + jnp.exp(rate * (-float(SEG * shift))) * earlier
            hseg[c, m] = jnp.where(segment >= 1, pltpu.roll(total, 1, 0), 0.0)
            est[c, spot, pl.ds(m, 1)] = total[SEGS - 1:]

    def send_states(c):
        block = est.at[c, spot]
        for device in mates:
            start(block, block, est_send.at[c], est_recv.at[c, spot], device)

    def slab_factor(c, slabs):
        return jnp.exp(decays[:, c * LANES:(c + 1) * LANES] * (-float(ROWS * slabs)))

    def plane_states(c):
        for place in mate_spots:
            copied(est.at[c, place], est_recv.at[c, place])
        factor = slab_factor(c, 1)
        total = est[c, 0]
        for q in range(1, 4):
            total = factor * total + est[c, q]
        pst[c, z] = total
        block = pst.at[c, z]

        def pass_on(later, _):
            start(block, block, pst_send.at[c, later], pst_recv.at[c, z], at(later, x, core, xhi, y))
            return 0

        lax.fori_loop(z + 1, PLANES, pass_on, 0)

    def finish(c):
        factor, plane_factor = slab_factor(c, 1), slab_factor(c, 4)

        def gather(earlier, total):
            copied(pst.at[c, earlier], pst_recv.at[c, earlier])
            return plane_factor * total + pst[c, earlier]

        total = lax.fori_loop(0, z, gather, jnp.zeros((MODES, LANES), F32))
        for q in range(3):
            total = jnp.where(q < spot, factor * total + est[c, q], total)
        segment = lax.broadcasted_iota(jnp.int32, (SEGS, LANES), 0).astype(F32)
        factors, states = [], []
        for m in range(MODES):
            rate, _ = mode_lanes(c, m)
            factors.append(jnp.exp(-rate))
            entering = jnp.exp(rate * (segment * -float(SEG))) * jnp.broadcast_to(total[m:m + 1], (SEGS, LANES))
            states.append(hseg[c, m] + entering)

        def step(i, states):
            states = tuple(f * s for f, s in zip(factors, states))
            parts = list(states)
            while len(parts) > 1:
                parts = [a + b for a, b in zip(parts[::2], parts[1::2])]
            place = pl.ds(i, SEGS, stride=SEG)
            ylocal[c, place, :] = ylocal[c, place, :] + parts[0]
            return states

        lax.fori_loop(0, SEG, step, tuple(states), unroll=4)
        value = sh0[c] * (ylocal[c] + lanes(skip, 0, c) * prod[c])
        gated[c, :, pl.ds(pl.multiple_of(chan * LANES, LANES), LANES)] = value.astype(BF16)

    def gate_slot(c, source):
        return gated.at[c, :, pl.ds(pl.multiple_of(source * LANES, LANES), LANES)]

    def send_gated(c, source, also_across):
        block = gate_slot(c, source)
        if also_across:
            start(block, block, gate_send.at[c], gate_recv.at[c, source], across)
        for y_ in y_mates:
            start(block, block, gate_send.at[c], gate_recv.at[c, source], at(z, x, core, xhi, y_))

    def relay_gated(c):
        source = (1 - xhi) * YS + y
        copied(gate_slot(c, source), gate_recv.at[c, source])
        send_gated(c, source, False)

    def add_out(c):
        for y_ in y_mates:
            for xhi_ in (xhi, 1 - xhi):
                source = xhi_ * YS + y_
                copied(gate_slot(c, source), gate_recv.at[c, source])
        part = jnp.dot(gated[c], wt[c], preferred_element_type=F32)
        if c == 0:
            acc[...] = part
        elif c < CHUNKS - 1:
            acc[...] += part
        else:
            out[...] = (acc[...] + part).astype(BF16)


    for c in range(CHUNKS):
        for j in range(3):
            pltpu.make_async_copy(
                w_in.at[j, :, c * LANES:(c + 1) * LANES],
                rows(c, z, x, core, 0, BLOCK).at[:, j * LANES:(j + 1) * LANES],
                local_sem.at[c],
            ).start()
    own_tokens = pltpu.make_async_copy(tokens, tok.at[pl.ds(HALO, ROWS)], local_sem.at[CHUNKS])
    own_tokens.start()
    own_columns = pltpu.make_async_copy(
        wt_columns(slice(None), chan), wt_slot(slice(None), chan), local_sem.at[CHUNKS + 1]
    )
    own_columns.start()

    barrier = pltpu.get_barrier_semaphore()
    greeted = planes + mates + [next_slab, prev_slab, across] + diagonals
    greeted += [at(z, x, core, xhi, y_) for y_ in y_mates]
    for device in greeted:
        pl.semaphore_signal(barrier, inc=1, device_id=device, device_id_type=MESH)
    pl.semaphore_wait(barrier, len(greeted))

    for c in range(CHUNKS):
        copied(main_rows(c, z), local_sem.at[c])

    def operator_parts(c):
        first = 2 * c + 6
        return {
            first: [lambda: (wait_w(c), project(c), shorten(c), recur(c), send_states(c))],
            first + 1: [lambda: plane_states(c)],
            first + 2: [lambda: (finish(c), send_gated(c, chan, True))],
            first + 3: [lambda: relay_gated(c)],
            first + 4: [lambda: add_out(c)],
        }

    work = {}
    for c in range(CHUNKS):
        for when, parts in operator_parts(c).items():
            work.setdefault(when, []).extend(parts)

    for t in range(2 * CHUNKS + 10):
        opened = t // 2 if t % 2 == 0 and t // 2 < CHUNKS else None
        if opened is not None:
            own_first(opened)
        for c in range(CHUNKS):
            if 1 <= t - 2 * c <= 4:
                ring(c, t - 2 * c)
        if opened is not None:
            own_second(opened)
        for c in range(CHUNKS):
            if 1 <= t - 2 * c <= 5:
                cross(c, t - 2 * c - 1)
        if t == 0:
            start(tokens.at[pl.ds(ROWS - HALO, HALO)], tok.at[pl.ds(0, HALO)], halo_sem.at[0], halo_sem.at[1], next_slab)
            wt_start()
        if t == 5:
            own_tokens.wait()
            copied(tok.at[pl.ds(0, HALO)], halo_sem.at[1])
        if t == 9:
            own_columns.wait()
            wt_relay()
            copied(wt.at[mine, pl.ds(0, 7 * LANES)], wt_core)
        for part in work.get(t, []):
            part()

    copied(tok.at[pl.ds(0, HALO)], halo_sem.at[0])
    copied(wt.at[mine, pl.ds(0, 7 * LANES)], wt_send)
    copied(wt.at[mine, pl.ds(0, 7 * LANES)], wt_core_send)
    for c in range(CHUNKS):
        copied(wbuf.at[c, pl.ds(0, 7 * (BLOCK + HALF) + 9 * HALF + DEPTH // 2)], w_send.at[c])
        copied(est.at[c, pl.ds(0, 3)], est_send.at[c])
        copied(gated.at[c, :, pl.ds(0, 7 * LANES)], gate_send.at[c])

        def sent(later, _):
            copied(pst.at[c, z], pst_send.at[c, later])
            return 0

        lax.fori_loop(z + 1, PLANES, sent, 0)


def body(tokens, w_in, short_taps, residues, decay_rates, skip_gain, w_out):
    any_space = pl.BlockSpec(memory_space=pl.ANY)
    vmem = pl.BlockSpec(memory_space=pltpu.VMEM)
    dma = pltpu.SemaphoreType.DMA
    width = CHUNKS * LANES
    return pl.pallas_call(
        kernel,
        out_shape=jax.ShapeDtypeStruct((ROWS, width), BF16),
        in_specs=[any_space, any_space, vmem, vmem, vmem, vmem, any_space],
        out_specs=vmem,
        scratch_shapes=[
            pltpu.VMEM((CHUNKS, DEPTH, WIDE), BF16),
            pltpu.VMEM((HALO + ROWS, DEPTH), BF16),
            pltpu.VMEM((CHUNKS, CHANS * LANES, width), BF16),
            pltpu.VMEM((HALO + ROWS, WIDE), F32),
            pltpu.VMEM((CHUNKS, ROWS, LANES), F32),
            pltpu.VMEM((CHUNKS, ROWS, LANES), F32),
            pltpu.VMEM((CHUNKS, ROWS, LANES), F32),
            pltpu.VMEM((CHUNKS, MODES, SEGS, LANES), F32),
            pltpu.VMEM((CHUNKS, 4, MODES, LANES), F32),
            pltpu.VMEM((CHUNKS, PLANES, MODES, LANES), F32),
            pltpu.VMEM((CHUNKS, ROWS, CHANS * LANES), BF16),
            pltpu.VMEM((ROWS, width), F32),
            dma((CHUNKS + 2,)),
            dma((CHUNKS,)),
            dma((CHUNKS, 4, 2)),
            dma((CHUNKS, 3, 2)),
            dma((CHUNKS, 8)),
            dma((CHUNKS,)),
            dma((CHUNKS,)),
            dma((2,)),
            dma((CHUNKS,)),
            dma((CHUNKS, 4)),
            dma((CHUNKS, PLANES)),
            dma((CHUNKS, PLANES)),
            dma((CHUNKS,)),
            dma((CHUNKS, CHANS)),
            dma,
            dma((CHANS,)),
            dma,
            dma,
        ],
        compiler_params=pltpu.CompilerParams(
            collective_id=0, has_side_effects=True, vmem_limit_bytes=56 << 20
        ),
        cost_estimate=pl.CostEstimate(flops=5 * 10**9, bytes_accessed=10**7, transcendentals=0),
        name="hyena",
    )(
        tokens,
        w_in.transpose(1, 0, 2),
        short_taps.reshape(9, width),
        residues,
        decay_rates,
        skip_gain.reshape(1, width),
        w_out,
    )


def solution(mesh):
    return jax.shard_map(
        body,
        mesh=mesh,
        in_specs=(
            P("seq", None),
            P("seq", None, "chan"),
            P(None, None, "chan"),
            P(None, "chan"),
            P(None, "chan"),
            P("chan"),
            P("chan", None),
        ),
        out_specs=P("seq", "chan"),
        check_vma=False,
    )
```

time: 565 us -> 102 us (0.18)
  waiting for transfers between devices: 304 us -> 0 us
  Pallas kernels: 0 us -> 97.4 us
  local copies, waits for them, and re-layouts: 90.5 us -> 3.03 us
  blocking collectives: 77.2 us -> 0 us
  matrix products: 47.2 us -> 0 us
  starting transfers between devices: 18 us -> 0 us
  between operations: 14.2 us -> 0.01 us
  other arithmetic: 8.16 us -> 0 us
    all_to_all x2 -> x0, waiting for transfers between devices: 121 us -> none  [regroup(): return lax.all_to_all(block, 'seq', split_axis=1, concat_axis=0, tiled=True)]
    all_gather x1 -> x0, waiting for transfers between devices: 108 us -> none  [body(): w_piece = lax.all_gather(w_in, 'seq', axis=0, tiled=True)]
    pallas_call x0 -> x1, Pallas kernels: none -> 97.4 us  [body(): pl.pallas_call(kernel, out_shape=jax.ShapeDtypeStruct((ROWS, width), BF16...]
    all_to_all x2 -> x0, blocking collectives: 77.2 us -> none  [regroup(): return lax.all_to_all(block, 'seq', split_axis=1, concat_axis=0, tiled=True)]
    reduce_scatter x1 -> x0, waiting for transfers between devices: 74.9 us -> none  [body(): lax.psum_scatter(partial_value.astype(jnp.bfloat16), 'chan', scatter_dime...]
    dot_general x14 -> x0, matrix products: 47.2 us -> none  [the longest x1 6.54 us: body(): jnp.dot(tokens, w_piece.reshape(w_piece.shape[0], -1), preferred_element_...]
    reshape x9 -> x1, local copies, waits for them, and re-layouts: 34.1 us -> 1.36 us  [body(): short_taps.reshape(9, width)]
    slice x7 -> x0, local copies, waits for them, and re-layouts: 30.6 us -> none  [the longest x2 13.6 us: forward_spectrum(): part_real = gathered[:, :, 0].reshape(tok_rows, -1)]
  transfers between devices with their start and end apart: 5 -> 0, of which waited for: 5 -> 0; matrix products, arithmetic and copies ran while one was open for 1% -> 0% of each run, Pallas kernels for 0% -> 0%
where the time goes in v1:
time: 102 us; the launch traced here: 100 us
  Pallas kernels  97.4 us (95%)
  local copies, waits for them, and re-layouts  3.03 us (3%)
    pallas_call x1, Pallas kernels, body(): pl.pallas_call(kernel, out_shape=jax.ShapeDtypeStruct((ROWS, width), BF16...  97.4 us

profile of v1, /device:TPU:1, one launch (start us, length us, event | category | flops | bytes accessed | tf_op | source)
XLA Modules:
  0.0 100.4 jit_solution(10983745019129952117)
XLA Ops:
  0.0 1.4 %reshape.6.taps = f32[9,512]{1,0:T(8,128)} reshape(f32[3,3,512]{2,1,0:T(4,128)} %param.9) | data formatting | bytes 36864 | tf_op jit(solution)/shard_map/reshape | solution.py:416
  1.4 97.4 %hyena.1 = bf16[256,512]{1,0:T(8,128)(2,1)} custom-call(bf16[256,4096]{1,0:T(8,128)(2,1)} %tokens.1, bf16[3,128,512]{2,1,0:T(8,128)(2,1)} %bitcast.2, f32[9,512]{1,0:T(8,128)} %reshape.6.taps, f32[16,512]{1,0:T(8,128)} %residues.1, f32[16,512]{1,0:T(8,128)} %decays.1, f32[1,512]{1,0:T(1,128)} %bitcast.3, bf16[512,4096]{1,0:T(8,128)(2,1)} %w_out.1), custom_call_target="tpu_custom_call" | custom-call | flops 5000000000 | bytes 10000000 | tf_op jit(solution)/shard_map/hyena/pallas_call | solution.py:371
  98.7 1.7 %copy.9 = bf16[256,512]{1,0:T(8,128)(2,1)} copy(bf16[256,512]{1,0:T(8,128)(2,1)} %hyena.1) | data formatting | bytes 524288

commit v2 on v1

v2 whole, which is shorter than its diff:
```python
import functools

import jax
import jax.numpy as jnp
from jax import lax
from jax.experimental import pallas as pl
from jax.experimental.pallas import tpu as pltpu
from jax.sharding import PartitionSpec as P

MESH = pl.DeviceIdType.MESH
F32, BF16 = jnp.float32, jnp.bfloat16

PLANES = 8
YS = 4
SLABS = 32
CHANS = 8
CHUNKS = 4
LANES = 128
WIDTH = CHUNKS * LANES
DEPTH = 4096
BLOCK = DEPTH // SLABS
HALF = BLOCK // 2
ROWS = 256
HALO = 16
SEGS = 8
SEG = ROWS // SEGS
MODES = 16
UNITS = (
    ((1, 2), 0, 1),
    ((1, 2), 1, 1),
    ((0,), 0, 1),
    ((1, 2), 2, 1),
    ((1, 2), 3, 1),
    ((0,), 1, 1),
    ((0,), 2, 1),
    ((0,), 3, 1),
)
OPENED = (0, 1, 2, 3, 4, 5, 6, 7)
STAGGERED = True
PLANE_LAG, ENTER_LAG, RELAY_LAG, OUT_LAG = 1, 2, 1, 2


def copied(ref, sem):
    pltpu.make_async_copy(ref, ref, sem).wait()


def kernel(
    tokens, w_in, taps_hbm, residues_hbm, decays_hbm, skip_hbm, w_out, out,
    taps, residues, decays, skip, wbufs, tok, wt, pj, sh0, prod, conv, hseg, est, pst, gated, acc,
    local_sem, w_send, w_major, w_minor, w_cross, w_inject, w_core, w_own,
    halo_sem, est_send, est_recv, pst_send, pst_recv, gate_send, gate_recv,
    wt_send, wt_recv, wt_core, wt_core_send,
):
    slab, chan = lax.axis_index("seq"), lax.axis_index("chan")
    z, spot = slab // 4, lax.rem(slab, 4)
    x, core = spot // 2, lax.rem(spot, 2)
    xhi, y = chan // YS, lax.rem(chan, YS)
    sign = 1 - 2 * core

    def at(z_, x_, core_, xhi_, y_):
        return (z_ * 4 + x_ * 2 + core_, xhi_ * YS + y_)

    def turned(distance):
        return lax.rem(z + distance * sign + 2 * PLANES, PLANES)

    ahead, behind = at(turned(1), x, core, xhi, y), at(turned(-1), x, core, xhi, y)
    beside, twin = at(z, 1 - x, core, xhi, y), at(z, x, 1 - core, xhi, y)
    across = at(z, x, core, 1 - xhi, y)
    mates = [at(z, x, 1 - core, xhi, y), at(z, 1 - x, core, xhi, y), at(z, 1 - x, 1 - core, xhi, y)]
    next_slab = (lax.rem(slab + 1, SLABS), chan)
    y_mates = [lax.rem(y + d, YS) for d in (1, 3, 2)]
    diagonals = [at(z, 1 - x, core, 1 - xhi, y_) for y_ in range(YS)]

    def start(src, dst, send, recv, device):
        pltpu.make_async_remote_copy(
            src_ref=src, dst_ref=dst, send_sem=send, recv_sem=recv, device_id=device, device_id_type=MESH
        ).start()


    def rows(c, z_, x_, core_, first, count):
        begin = pl.multiple_of((z_ * 4 + x_ * 2 + core_) * BLOCK + first, HALF)
        return wbufs[c].at[pl.ds(begin, count)]

    def w_copy(c, ref, device, recv):
        start(ref, ref, w_send.at[c], recv, device)

    def main_rows(c, z_):
        return rows(c, z_, x, core, 0, BLOCK)

    def carried_rows(c, z_):
        return rows(c, z_, 1 - x, core, 0, HALF)

    def to_core(c, ref):
        w_copy(c, ref, twin, w_core.at[c])

    def inject(c):
        w_copy(c, rows(c, z, x, core, 0, HALF), beside, w_inject.at[c])

    def own_first(c):
        block = main_rows(c, z)
        start(block, block, w_own.at[c], w_major.at[c, 0, 0], ahead)
        start(block, block, w_own.at[c], w_minor.at[c, 0, 0], behind)
        w_copy(c, rows(c, z, x, core, HALF, HALF), beside, w_cross.at[c])
        to_core(c, main_rows(c, z))

    def own_sent(c):
        copied(wbufs[c].at[pl.ds(0, 2 * BLOCK)], w_own.at[c])

    def own_second(c):
        block = carried_rows(c, z)
        copied(block, w_inject.at[c])
        w_copy(c, block, ahead, w_major.at[c, 0, 1])
        w_copy(c, block, behind, w_minor.at[c, 0, 1])
        to_core(c, block)

    def ring(c, j):
        for part, of in ((0, main_rows), (1, carried_rows)):
            for sems, device, last, source in (
                (w_major, ahead, 4, turned(-j)),
                (w_minor, behind, 3, turned(j)),
            ):
                if j > last:
                    continue
                block = of(c, source)
                copied(block, sems.at[c, j - 1, part])
                if j < last:
                    w_copy(c, block, device, sems.at[c, j, part])
                if part == 0:
                    w_copy(c, rows(c, source, x, core, HALF, HALF), beside, w_cross.at[c])
                to_core(c, block)

    def cross(c):
        copied(wbufs[c].at[pl.ds(0, PLANES * HALF)], w_cross.at[c])
        for source in range(PLANES):
            to_core(c, rows(c, source, 1 - x, core, HALF, HALF))


    w_out_chunks = w_out.reshape(CHUNKS, LANES, DEPTH)
    mine = pl.ds(core * 2, 2)

    def wt_slot(part, source):
        return wt.at[part, pl.ds(pl.multiple_of(source * LANES, LANES), LANES)]

    def wt_columns(part, target):
        return w_out_chunks.at[part, :, pl.ds(pl.multiple_of(target * 512, 512), 512)]

    wt_peers = [(xhi * YS + y_, at(z, x, core, xhi, y_)) for y_ in y_mates]
    wt_peers += [((1 - xhi) * YS + y_, diagonals[y_]) for y_ in range(YS)]

    def wt_start():
        for target, device in wt_peers:
            start(wt_columns(mine, target), wt_slot(mine, chan), wt_send, wt_recv, device)

    def wt_relay():
        copied(wt.at[mine, pl.ds(0, 7 * LANES)], wt_recv)
        for source, _ in wt_peers:
            start(wt_slot(mine, source), wt_slot(mine, source), wt_core_send, wt_core, twin)


    def lanes(ref, row, c):
        return ref[pl.ds(row, 1), c * LANES:(c + 1) * LANES]

    def project(u):
        copied(wbufs[u].at[pl.ds(0, DEPTH // 2)], w_core.at[u])
        width = wbufs[u].shape[1]
        result = jnp.dot(tok[...], wbufs[u][...], preferred_element_type=F32)
        pj[:, :width] = result.astype(BF16).astype(F32)

        @pl.when(slab == 0)
        def _():
            pj[pl.ds(0, HALO), :width] = jnp.zeros((HALO, width), F32)

        streams, first, count = UNITS[u]

        def shorted(j, c):
            column = streams.index(j) * count + c - first
            total = None
            for a in range(3):
                tap = taps[a, pl.ds(j, 1), c * LANES:(c + 1) * LANES]
                term = tap * pj[pl.ds(HALO - a, ROWS), column * LANES:(column + 1) * LANES]
                total = term if total is None else total + term
            return total

        for c in range(first, first + count):
            if 0 in streams:
                sh0[c] = shorted(0, c)
            if 1 in streams:
                prod[c] = shorted(1, c) * shorted(2, c)
                recur(c)
                send_states(c)

    def mode_lanes(c, m):
        rate = jnp.broadcast_to(lanes(decays, m, c), (SEGS, LANES))
        size = jnp.broadcast_to(lanes(residues, m, c), (SEGS, LANES))
        return rate, size

    def added(parts):
        parts = list(parts)
        while len(parts) > 1:
            parts = [a + b for a, b in zip(parts[::2], parts[1::2])]
        return parts[0]

    def recur(c):
        factors, gains = [], []
        for m in range(MODES):
            rate, size = mode_lanes(c, m)
            factors.append(jnp.exp(-rate))
            gains.append(size * jnp.sqrt(rate * (2.0 / MODES)))

        def step(i, states):
            place = pl.ds(i, SEGS, stride=SEG)
            value = prod[c, place, :]
            states = tuple(f * s + g * value for f, g, s in zip(factors, gains, states))
            conv[c, place, :] = added(states)
            return states

        states = lax.fori_loop(0, SEG, step, (jnp.zeros((SEGS, LANES), F32),) * MODES, unroll=4)
        segment = lax.broadcasted_iota(jnp.int32, (SEGS, LANES), 0)
        for m in range(MODES):
            rate, _ = mode_lanes(c, m)
            total = states[m]
            for shift in (1, 2, 4):
                earlier = jnp.where(segment >= shift, pltpu.roll(total, shift, 0), 0.0)
                total = total + jnp.exp(rate * (-float(SEG * shift))) * earlier
            hseg[c, m] = jnp.where(segment >= 1, pltpu.roll(total, 1, 0), 0.0)
            est[c, spot, pl.ds(m, 1)] = total[SEGS - 1:]

    def send_states(c):
        block = est.at[c, spot]
        for device in mates:
            start(block, block, est_send.at[c], est_recv.at[c], device)

    def slab_factor(c, slabs):
        return jnp.exp(decays[:, c * LANES:(c + 1) * LANES] * (-float(ROWS * slabs)))

    def plane_states(c):
        copied(est.at[c, pl.ds(0, 3)], est_recv.at[c])
        factor = slab_factor(c, 1)
        total = est[c, 0]
        for q in range(1, 4):
            total = factor * total + est[c, q]
        pst[c, z] = total
        block = pst.at[c, z]

        for d in (4, 3, 5, 2, 6, 1, 7):
            device = at(lax.rem(z + d, PLANES), x, core, xhi, y)
            start(block, block, pst_send.at[c], pst_recv.at[c], device)

    def enter(c):
        factor, plane_factor = slab_factor(c, 1), slab_factor(c, 4)

        copied(pst.at[c, pl.ds(0, PLANES - 1)], pst_recv.at[c])
        total = jnp.zeros((MODES, LANES), F32)
        for earlier in range(PLANES - 1):
            total = jnp.where(earlier < z, plane_factor * total + pst[c, earlier], total)
        for q in range(3):
            total = jnp.where(q < spot, factor * total + est[c, q], total)
        segment = lax.broadcasted_iota(jnp.int32, (SEGS, LANES), 0).astype(F32)
        factors, states = [], []
        for m in range(MODES):
            rate, _ = mode_lanes(c, m)
            factors.append(jnp.exp(-rate))
            entering = jnp.broadcast_to(total[m:m + 1], (SEGS, LANES))
            states.append(hseg[c, m] + jnp.exp(rate * (segment * -float(SEG))) * entering)

        def step(i, states):
            states = tuple(f * s for f, s in zip(factors, states))
            place = pl.ds(i, SEGS, stride=SEG)
            conv[c, place, :] = conv[c, place, :] + added(states)
            return states

        lax.fori_loop(0, SEG, step, tuple(states), unroll=4)
        conv[c] = conv[c] + lanes(skip, 0, c) * prod[c]

    def gate_slot(c, source):
        return gated.at[c, :, pl.ds(pl.multiple_of(source * LANES, LANES), LANES)]


    def send_across(c, source, part):
        block = gate_slot(c, source)
        start(block, block, gate_send.at[c], gate_recv.at[c, part], across)

    def send_along(c, source, part):
        block = gate_slot(c, source)
        for y_ in y_mates:
            start(block, block, gate_send.at[c], gate_recv.at[c, part], at(z, x, core, xhi, y_))

    def gate(c):
        gated[c, :, pl.ds(pl.multiple_of(chan * LANES, LANES), LANES)] = (sh0[c] * conv[c]).astype(BF16)

        @pl.when(core == 0)
        def _():
            send_across(c, chan, 0)
            send_along(c, chan, 1)

        @pl.when(core == 1)
        def _():
            send_along(c, chan, 0)
            send_across(c, chan, 1)

    def gated_here(c, part, blocks):
        copied(gated.at[c, :, pl.ds(0, blocks * LANES)], gate_recv.at[c, part])

    def relay_gated(c):
        @pl.when(core == 0)
        def _():
            gated_here(c, 0, 1)
            send_along(c, (1 - xhi) * YS + y, 1)

        @pl.when(core == 1)
        def _():
            gated_here(c, 0, 3)
            for y_ in y_mates:
                send_across(c, xhi * YS + y_, 1)

    def add_out(c):
        @pl.when(core == 0)
        def _():
            gated_here(c, 1, 6)

        @pl.when(core == 1)
        def _():
            gated_here(c, 1, 4)

        part = jnp.dot(gated[c], wt[c], preferred_element_type=F32)
        if c == 0:
            acc[...] = part
        elif c < CHUNKS - 1:
            acc[...] += part
        else:
            out[...] = (acc[...] + part).astype(BF16)


    units = range(len(UNITS))
    for u, (streams, first, count) in enumerate(UNITS):
        for i, j in enumerate(streams):
            width = count * LANES
            pltpu.make_async_copy(
                w_in.at[j, :, first * LANES:first * LANES + width],
                rows(u, z, x, core, 0, BLOCK).at[:, i * width:(i + 1) * width],
                local_sem.at[0],
            ).start()
    own_tokens = pltpu.make_async_copy(tokens, tok.at[pl.ds(HALO, ROWS)], local_sem.at[1])
    own_tokens.start()
    own_columns = pltpu.make_async_copy(
        wt_columns(slice(None), chan), wt_slot(slice(None), chan), local_sem.at[2]
    )
    own_columns.start()
    parameters = [
        pltpu.make_async_copy(src, dst, local_sem.at[3 + i])
        for i, (src, dst) in enumerate(
            ((taps_hbm, taps), (residues_hbm, residues), (decays_hbm, decays), (skip_hbm, skip))
        )
    ]
    for copy in parameters:
        copy.start()

    barrier = pltpu.get_barrier_semaphore()
    planes = [at(lax.rem(z + d, PLANES), x, core, xhi, y) for d in (4, 3, 5, 2, 6, 1, 7)]
    greeted = planes + diagonals + [across] + [at(z, x, core, xhi, y_) for y_ in y_mates] + mates
    greeted += [next_slab, (lax.rem(slab + SLABS - 1, SLABS), chan)]
    for device in greeted:
        pl.semaphore_signal(barrier, inc=1, device_id=device, device_id_type=MESH)
    pl.semaphore_wait(barrier, len(greeted))

    def start_columns():
        start(tokens.at[pl.ds(ROWS - HALO, HALO)], tok.at[pl.ds(0, HALO)], halo_sem.at[0], halo_sem.at[1], next_slab)
        wt_start()

    copied(wbufs[0].at[pl.ds(0, BLOCK * 3 * WIDTH // wbufs[0].shape[1])], local_sem.at[0])

    def halo_here():
        own_tokens.wait()
        for copy in parameters:
            copy.wait()
        copied(tok.at[pl.ds(0, HALO)], halo_sem.at[1])

    def columns_here():
        own_columns.wait()
        wt_relay()
        copied(wt.at[mine, pl.ds(0, 7 * LANES)], wt_core)

    work = {}

    def plan(when, rank, part):
        work.setdefault(when, []).append((rank, len(work.get(when, [])), part))

    def unit_of(stream, c):
        return next(u for u in units if stream in UNITS[u][0] and UNITS[u][1] <= c < UNITS[u][1] + UNITS[u][2])

    plan(0, 0, start_columns)
    plan(OPENED[0] + 5, 0, halo_here)
    for u in units:
        plan(OPENED[u] + 5, 1 + u, functools.partial(project, u))
    last = 0
    for c in range(CHUNKS):
        when = OPENED[unit_of(1, c)] + 5 + PLANE_LAG
        plan(when, 0, functools.partial(plane_states, c))
        when += ENTER_LAG
        plan(when, 20, functools.partial(enter, c))
        u = unit_of(0, c)
        rank = 21
        if OPENED[u] + 5 > when:
            when, rank = OPENED[u] + 5, 1.5 + u
        plan(when, rank, functools.partial(gate, c))
        plan(when + RELAY_LAG, 30 + c, functools.partial(relay_gated, c))
        last = max(last + 1, when + OUT_LAG)
        plan(last, 40 + c, functools.partial(add_out, c))
        if c == 0:
            plan(last, 0, columns_here)

    for t in range(last + 1):
        opened = [u for u in units if OPENED[u] == t]
        if t == 0:
            for u in units:
                inject(u)
        for u in opened:
            if u > opened[0] and STAGGERED:
                own_sent(u - 1)
            own_first(u)
            if STAGGERED:
                own_second(u)
        for u in units:
            if 1 <= t - OPENED[u] <= 4:
                ring(u, t - OPENED[u])
        for u in opened:
            if not STAGGERED:
                own_second(u)
        for u in units:
            if t - OPENED[u] == 5:
                cross(u)
        for _, _, part in sorted(work.get(t, []), key=lambda entry: entry[:2]):
            part()

    copied(tok.at[pl.ds(0, HALO)], halo_sem.at[0])
    copied(wt.at[mine, pl.ds(0, 7 * LANES)], wt_send)
    copied(wt.at[mine, pl.ds(0, 7 * LANES)], wt_core_send)
    for u in units:
        if not (STAGGERED and u + 1 < len(UNITS) and OPENED[u + 1] == OPENED[u]):
            own_sent(u)
        copied(wbufs[u].at[pl.ds(0, 5 * BLOCK + 7 * HALF + 9 * HALF + DEPTH // 2)], w_send.at[u])
    for c in range(CHUNKS):
        copied(gated.at[c, :, pl.ds(0, 7 * LANES)], gate_send.at[c])
        copied(est.at[c, pl.ds(0, 3)], est_send.at[c])
        copied(pst.at[c, pl.ds(0, PLANES - 1)], pst_send.at[c])


def body(tokens, w_in, short_taps, residues, decay_rates, skip_gain, w_out):
    any_space = pl.BlockSpec(memory_space=pl.ANY)
    vmem = pl.BlockSpec(memory_space=pltpu.VMEM)
    dma = pltpu.SemaphoreType.DMA
    units = len(UNITS)
    return pl.pallas_call(
        kernel,
        out_shape=jax.ShapeDtypeStruct((ROWS, WIDTH), BF16),
        in_specs=[any_space] * 7,
        out_specs=vmem,
        scratch_shapes=[
            pltpu.VMEM((3, 3, WIDTH), F32),
            pltpu.VMEM((MODES, WIDTH), F32),
            pltpu.VMEM((MODES, WIDTH), F32),
            pltpu.VMEM((1, WIDTH), F32),
            [pltpu.VMEM((DEPTH, len(streams) * count * LANES), BF16) for streams, _, count in UNITS],
            pltpu.VMEM((HALO + ROWS, DEPTH), BF16),
            pltpu.VMEM((CHUNKS, CHANS * LANES, WIDTH), BF16),
            pltpu.VMEM((HALO + ROWS, WIDTH), F32),
            pltpu.VMEM((CHUNKS, ROWS, LANES), F32),
            pltpu.VMEM((CHUNKS, ROWS, LANES), F32),
            pltpu.VMEM((CHUNKS, ROWS, LANES), F32),
            pltpu.VMEM((CHUNKS, MODES, SEGS, LANES), F32),
            pltpu.VMEM((CHUNKS, 4, MODES, LANES), F32),
            pltpu.VMEM((CHUNKS, PLANES, MODES, LANES), F32),
            pltpu.VMEM((CHUNKS, ROWS, CHANS * LANES), BF16),
            pltpu.VMEM((ROWS, WIDTH), F32),
            dma((7,)),
            dma((units,)),
            dma((units, 4, 2)),
            dma((units, 3, 2)),
            dma((units,)),
            dma((units,)),
            dma((units,)),
            dma((units,)),
            dma((2,)),
            dma((CHUNKS,)),
            dma((CHUNKS,)),
            dma((CHUNKS,)),
            dma((CHUNKS,)),
            dma((CHUNKS,)),
            dma((CHUNKS, 2)),
            dma,
            dma,
            dma,
            dma,
        ],
        compiler_params=pltpu.CompilerParams(
            collective_id=0, has_side_effects=True, vmem_limit_bytes=56 << 20
        ),
        cost_estimate=pl.CostEstimate(flops=5 * 10**9, bytes_accessed=10**7, transcendentals=0),
        name="hyena",
    )(
        tokens,
        w_in.transpose(1, 0, 2),
        short_taps,
        residues,
        decay_rates,
        skip_gain.reshape(1, WIDTH),
        w_out,
    )


def solution(mesh):
    return jax.shard_map(
        body,
        mesh=mesh,
        in_specs=(
            P("seq", None),
            P("seq", None, "chan"),
            P(None, None, "chan"),
            P(None, "chan"),
            P(None, "chan"),
            P("chan"),
            P("chan", None),
        ),
        out_specs=P("seq", "chan"),
        check_vma=False,
    )
```

time: 102 us -> 93.1 us (0.913); the launches traced: 100 us -> 93 us
  Pallas kernels: 97.4 us -> 91.3 us
  local copies, waits for them, and re-layouts: 3.03 us -> 1.67 us
    pallas_call x1, Pallas kernels: 97.4 us -> 91.3 us  [body(): pl.pallas_call(kernel, out_shape=jax.ShapeDtypeStruct((ROWS, WIDTH), BF16...]
    reshape x1 -> x0, local copies, waits for them, and re-layouts: 1.36 us -> none  [body(): short_taps.reshape(9, width)]
where the time goes in v2:
time: 93.1 us; the launch traced here: 93 us
  Pallas kernels  91.3 us (98%)
  local copies, waits for them, and re-layouts  1.67 us (2%)
    pallas_call x1, Pallas kernels, body(): pl.pallas_call(kernel, out_shape=jax.ShapeDtypeStruct((ROWS, WIDTH), BF16...  91.3 us

profile of v2, /device:TPU:1, one launch (start us, length us, event | category | flops | bytes accessed | tf_op | source)
XLA Modules:
  0.0 93.0 jit_solution(14304303399541929346)
XLA Ops:
  0.0 91.3 %hyena.1 = bf16[256,512]{1,0:T(8,128)(2,1)} custom-call(bf16[256,4096]{1,0:T(8,128)(2,1)} %tokens.1, bf16[3,128,512]{2,1,0:T(8,128)(2,1)} %bitcast.2, f32[3,3,512]{2,1,0:T(4,128)} %taps_hbm.1, f32[16,512]{1,0:T(8,128)} %residues_hbm.1, f32[16,512]{1,0:T(8,128)} %decays_hbm.1, f32[1,512]{1,0:T(1,128)} %bitcast.3, bf16[512,4096]{1,0:T(8,128)(2,1)} %w_out.1), custom_call_target="tpu_custom_call" | custom-call | flops 5000000000 | bytes 10000000 | tf_op jit(solution)/shard_map/hyena/pallas_call | solution.py:453
  91.3 1.7 %copy.9 = bf16[256,512]{1,0:T(8,128)(2,1)} copy(bf16[256,512]{1,0:T(8,128)(2,1)} %hyena.1) | data formatting | bytes 524288

commit v3 on v2

--- a/solution.py
+++ b/solution.py
@@ -377,7 +377,6 @@
 
     def columns_here():
         own_columns.wait()
-        wt_relay()
         copied(wt.at[mine, pl.ds(0, 7 * LANES)], wt_core)
 
     work = {}
@@ -404,10 +403,11 @@
             when, rank = OPENED[u] + 5, 1.5 + u
         plan(when, rank, functools.partial(gate, c))
         plan(when + RELAY_LAG, 30 + c, functools.partial(relay_gated, c))
-        last = max(last + 1, when + OUT_LAG)
+        last = max(last, when + OUT_LAG)
+    plan(OPENED[0] + 8, 25, wt_relay)
+    plan(last, 39, columns_here)
+    for c in range(CHUNKS):
         plan(last, 40 + c, functools.partial(add_out, c))
-        if c == 0:
-            plan(last, 0, columns_here)
 
     for t in range(last + 1):
         opened = [u for u in units if OPENED[u] == t]

time: 93.1 us -> 91.3 us (0.981)
  Pallas kernels: 91.3 us -> 89.5 us
    pallas_call x1, Pallas kernels: 91.3 us -> 89.5 us  [body(): pl.pallas_call(kernel, out_shape=jax.ShapeDtypeStruct((ROWS, WIDTH), BF16...]
where the time goes in v3:
time: 91.3 us; the launch traced here: 91.2 us
  Pallas kernels  89.5 us (98%)
  local copies, waits for them, and re-layouts  1.67 us (2%)
    pallas_call x1, Pallas kernels, body(): pl.pallas_call(kernel, out_shape=jax.ShapeDtypeStruct((ROWS, WIDTH), BF16...  89.5 us

profile of v3, /device:TPU:1, one launch (start us, length us, event | category | flops | bytes accessed | tf_op | source)
XLA Modules:
  0.0 91.2 jit_solution(9167148649377991649)
XLA Ops:
  0.0 89.5 %hyena.1 = bf16[256,512]{1,0:T(8,128)(2,1)} custom-call(bf16[256,4096]{1,0:T(8,128)(2,1)} %tokens.1, bf16[3,128,512]{2,1,0:T(8,128)(2,1)} %bitcast.2, f32[3,3,512]{2,1,0:T(4,128)} %taps_hbm.1, f32[16,512]{1,0:T(8,128)} %residues_hbm.1, f32[16,512]{1,0:T(8,128)} %decays_hbm.1, f32[1,512]{1,0:T(1,128)} %bitcast.3, bf16[512,4096]{1,0:T(8,128)(2,1)} %w_out.1), custom_call_target="tpu_custom_call" | custom-call | flops 5000000000 | bytes 10000000 | tf_op jit(solution)/shard_map/hyena/pallas_call | solution.py:453
  89.5 1.7 %copy.9 = bf16[256,512]{1,0:T(8,128)(2,1)} copy(bf16[256,512]{1,0:T(8,128)(2,1)} %hyena.1) | data formatting | bytes 524288
